TPU v7x, 128 devices: a whole 4x4x4 slice. The times are simulated.
128 devices in a mesh: leaf: 128 (over y, z, x, core).
Axes of the slice: x: 4, y: 4, z: 4, core: 2. Of those that a mesh axis runs over, the one named last changes fastest.
Arguments:
- points: bfloat16 [4096, 32, 256], P('leaf'), may hold values from -6 to 6
- weights: bfloat16 [4096, 4, 256], P('leaf'), may hold values from -6 to 6
- leaf_maps: bfloat16 [4096, 128, 256], P('leaf'), may hold values from -0.375 to 0.375
- root_maps: bfloat16 [128, 128, 4096], P('leaf'), may hold values from -0.09375 to 0.09375
- top_maps: bfloat16 [128, 128, 256], P('leaf'), may hold values from -0.375 to 0.375
- root_picks: int32 [128, 128], P('leaf'), may hold values from 0 to 8191
- top_picks: int32 [128, 128], P('leaf'), may hold values from 0 to 255
- near_lists: int32 [4096, 16], P('leaf'), may hold values from 0 to 4095, as said below
- far_lists: int32 [4096, 32], P('leaf'), may hold values from 1 to 255
Outputs:
- product: float32 [4096, 4, 256], P('leaf')
Inputs may be any that keep to these rules, and one draw needn't show every extreme that they name: near_lists[g, 0] = g, and every entry lies within 32 leaves of g; entries may repeat.
All inputs are finite; a program needn't handle non-finite values.
Results may differ from a plain program's by a relative error of at most 0.008.
Values may be sent and summed in bfloat16 or wider, within the bound.
No kernel may reach another device: no remote copies, remote signals or barrier semaphores. Data moves between devices by JAX's collectives and lax.ppermute only.
A program may use at most 64 MiB of HBM per device.

v0:
```python
import jax
import jax.numpy as jnp
from jax import lax
from jax.sharding import PartitionSpec as P

gauss = 0.0625


def padded_2(shard, sides, width):
    for axis, dim in sides:
        size, length = (lax.axis_size(axis), shard.shape[dim])
        up = [(i, (i + 1) % size) for i in range(size - 1)]
        down = [(j, i) for i, j in up]
        last = lax.slice_in_dim(shard, length - width, length, axis=dim)
        initial = lax.slice_in_dim(shard, 0, width, axis=dim)
        before = lax.ppermute(last, axis, up)
        after = lax.ppermute(initial, axis, down)
        shard = jnp.concatenate([before, shard, after], axis=dim)
    return shard


def kernel_apply(targets, sources, source_w):
    cross = jnp.einsum("dt,mds->tms", targets, sources, preferred_element_type=jnp.float32)
    tnorm = jnp.sum(jnp.square(targets.astype(jnp.float32)), axis=0)
    snorm = jnp.sum(jnp.square(sources.astype(jnp.float32)), axis=1)
    kern = jnp.exp(-gauss * (tnorm[:, None, None] + snorm[None] - 2.0 * cross)).astype(jnp.bfloat16)
    return jnp.einsum("tms,mrs->rt", kern, source_w, preferred_element_type=jnp.float32)


def merge_level(cur_w, cur_x, maps, picks, half):
    rhs = cur_w.shape[1]
    dims = cur_x.shape[1]
    rank = cur_w.shape[2]
    pair_w = cur_w.reshape(half, 2, rhs, rank).transpose(0, 2, 1, 3).reshape(half, rhs, 2 * rank)
    pair_x = cur_x.reshape(half, 2, dims, rank).transpose(0, 2, 1, 3).reshape(half, dims, 2 * rank)
    new_w = jnp.einsum(
        "nrk,nsk->nrs", pair_w, maps.astype(jnp.float32), precision=lax.Precision.HIGHEST
    )
    new_x = jnp.take_along_axis(pair_x, picks[:, None, :], axis=2)
    return (new_w, new_x)


def collect_level(own_w, own_x):
    return (
        lax.all_gather(own_w[None], "leaf", axis=0, tiled=True),
        lax.all_gather(own_x[None], "leaf", axis=0, tiled=True),
    )


def on_device(
    points, weights, leaf_maps, root_maps, top_maps, root_picks, top_picks, near_lists, far_lists
):
    per = points.shape[0]
    dims = points.shape[1]
    leaf_size = points.shape[2]
    rhs = weights.shape[1]
    rank = leaf_maps.shape[1]
    nodes = lax.axis_size("leaf")
    me = lax.axis_index("leaf")
    high = lax.Precision.HIGHEST
    leaf_w = jnp.einsum("grp,gsp->grs", weights, leaf_maps, preferred_element_type=jnp.float32)
    stacked = leaf_w.transpose(1, 0, 2).reshape(rhs, per * rank)
    root_w = jnp.dot(stacked, root_maps[0].astype(jnp.float32).T, precision=high)
    flat = points.transpose(1, 0, 2).reshape(dims, per * leaf_size)
    root_x = jnp.take(flat, root_picks[0], axis=1).astype(jnp.float32)
    own_w, own_x = (root_w, root_x)
    gathered_w = []
    gathered_x = []
    depth = nodes.bit_length() - 1
    count = nodes
    for level_step in range(depth):
        all_w, all_x = collect_level(own_w, own_x)
        gathered_w.append(all_w)
        gathered_x.append(all_x)
        half = count // 2
        first = 2 * me - nodes if count == nodes else 2 * me
        first = jnp.clip(first, 0, nodes - 2)
        pair_w = lax.dynamic_slice_in_dim(all_w, first, 2, 0)
        pair_x = lax.dynamic_slice_in_dim(all_x, first, 2, 0)
        new_w, new_x = merge_level(pair_w, pair_x, top_maps, top_picks, 1)
        owner = jnp.logical_and(me >= half, me < count)
        own_w = jnp.where(owner, new_w[0], 0.0)
        own_x = jnp.where(owner, new_x[0], 0.0)
        count = half
    all_w, all_x = collect_level(own_w, own_x)
    gathered_w.append(all_w)
    gathered_x.append(all_x)
    pieces_w = [jnp.zeros((1, rhs, rank), jnp.float32)]
    pieces_x = [jnp.zeros((1, dims, rank), jnp.float32)]
    for level in range(len(gathered_w) - 1, 0, -1):
        lower = nodes >> level
        upper = nodes >> level - 1
        pieces_w.append(gathered_w[level][lower:upper])
        pieces_x.append(gathered_x[level][lower:upper])
    pieces_w.append(gathered_w[0])
    pieces_x.append(gathered_x[0])
    table_w = jnp.concatenate(pieces_w, axis=0)
    table_x = jnp.concatenate(pieces_x, axis=0)
    table_wb = table_w.astype(jnp.bfloat16)
    table_xb = table_x.astype(jnp.bfloat16)
    joined = jnp.concatenate([points, weights], axis=1)
    padded = padded_2(joined, (("leaf", 0),), per)
    near_local = near_lists - (me * per - per)

    def one_leaf(target, near_ids, far_ids):
        sources = padded[near_ids]
        near = kernel_apply(target, sources[:, :dims], sources[:, dims:])
        far = kernel_apply(target, table_xb[far_ids], table_wb[far_ids])
        return near + far

    def pair_leaves(args):
        return jax.vmap(one_leaf)(*args)

    grouped = (
        points.reshape(per // 2, 2, dims, leaf_size),
        near_local.reshape(per // 2, 2, -1),
        far_lists.reshape(per // 2, 2, -1),
    )
    result = lax.map(pair_leaves, grouped)
    return result.reshape(per, rhs, leaf_size)


def solution(mesh):
    in_specs = (
        P("leaf", None, None),
        P("leaf", None, None),
        P("leaf", None, None),
        P("leaf", None, None),
        P("leaf", None, None),
        P("leaf", None),
        P("leaf", None),
        P("leaf", None),
        P("leaf", None),
    )
    out_specs = P("leaf", None, None)
    return jax.shard_map(
        on_device, mesh=mesh, in_specs=in_specs, out_specs=out_specs, check_vma=False
    )
```

profile of v0, /device:TPU:0, one launch (start us, length us, event | category | flops | bytes accessed | tf_op | source)
XLA Modules:
  0.0 972.9 jit_solution(13773557444124703738)
XLA Ops:
  14.1 66.0 %all-gather.25.cloned.1.call-done = bf16[128,32,128]{2,1,0:T(8,128)(2,1)} async-done(((bf16[1,32,128]{2,1,0:T(8,128)(2,1)}), bf16[128,32,128]{2,1,0:T(8,128)(2,1)}) %all-gather.25.cloned.1.call-update) | async-done | bytes 1048592 | tf_op jit(solution)/shard_map/all_gather | solution.py:46
  82.6 61.4 %all-gather.27.cloned.1.call-done = bf16[128,32,128]{2,1,0:T(8,128)(2,1)} async-done(((bf16[1,32,128]{2,1,0:T(8,128)(2,1)}), bf16[128,32,128]{2,1,0:T(8,128)(2,1)}) %all-gather.27.cloned.1.call-update) | async-done | bytes 1048592 | tf_op jit(solution)/shard_map/all_gather | solution.py:46
  146.4 61.4 %all-gather.29.cloned.1.call-done = bf16[128,32,128]{2,1,0:T(8,128)(2,1)} async-done(((bf16[1,32,128]{2,1,0:T(8,128)(2,1)}), bf16[128,32,128]{2,1,0:T(8,128)(2,1)}) %all-gather.29.cloned.1.call-update) | async-done | bytes 1048592 | tf_op jit(solution)/shard_map/all_gather | solution.py:46
  210.3 61.3 %all-gather.31.cloned.1.call-done = bf16[128,32,128]{2,1,0:T(8,128)(2,1)} async-done(((bf16[1,32,128]{2,1,0:T(8,128)(2,1)}), bf16[128,32,128]{2,1,0:T(8,128)(2,1)}) %all-gather.31.cloned.1.call-update) | async-done | bytes 1048592 | tf_op jit(solution)/shard_map/all_gather | solution.py:46
  274.0 61.3 %all-gather.33.cloned.1.call-done = bf16[128,32,128]{2,1,0:T(8,128)(2,1)} async-done(((bf16[1,32,128]{2,1,0:T(8,128)(2,1)}), bf16[128,32,128]{2,1,0:T(8,128)(2,1)}) %all-gather.33.cloned.1.call-update) | async-done | bytes 1048592 | tf_op jit(solution)/shard_map/all_gather | solution.py:46
  338.0 3.0 collective-permute-start
  344.5 54.5 %all-gather.35.cloned.1.call-done = bf16[128,32,128]{2,1,0:T(8,128)(2,1)} async-done(((bf16[1,32,128]{2,1,0:T(8,128)(2,1)}), bf16[128,32,128]{2,1,0:T(8,128)(2,1)}) %all-gather.35.cloned.1.call-update) | async-done | bytes 1048592 | tf_op jit(solution)/shard_map/all_gather | solution.py:46
  401.4 33.4 %all-gather.8 = f32[128,4,128]{2,1,0:T(4,128)S(1)} all-gather(f32[1,4,128]{2,1,0:T(4,128)S(1)} %convolution_bitcast_fusion.1), channel_id=2, replica_groups=mesh['leaf'=128] {'leaf'}, dimensions={0}, use_global_device_ids=true | all-gather | bytes 264192 | tf_op jit(solution)/shard_map/all_gather | solution.py:45
  435.0 33.3 %all-gather.9 = f32[128,4,128]{2,1,0:T(4,128)S(1)} all-gather(f32[1,4,128]{2,1,0:T(4,128)S(1)} %fusion.36), channel_id=3, replica_groups=mesh['leaf'=128] {'leaf'}, dimensions={0}, use_global_device_ids=true | all-gather | bytes 264192 | tf_op jit(solution)/shard_map/all_gather | solution.py:45
  468.4 33.3 %all-gather.10 = f32[128,4,128]{2,1,0:T(4,128)S(1)} all-gather(f32[1,4,128]{2,1,0:T(4,128)S(1)} %fusion.35), channel_id=4, replica_groups=mesh['leaf'=128] {'leaf'}, dimensions={0}, use_global_device_ids=true | all-gather | bytes 264192 | tf_op jit(solution)/shard_map/all_gather | solution.py:45
  501.7 33.3 %all-gather.11 = f32[128,4,128]{2,1,0:T(4,128)S(1)} all-gather(f32[1,4,128]{2,1,0:T(4,128)S(1)} %fusion.34), channel_id=5, replica_groups=mesh['leaf'=128] {'leaf'}, dimensions={0}, use_global_device_ids=true | all-gather | bytes 264192 | tf_op jit(solution)/shard_map/all_gather | solution.py:45
  535.1 33.3 %all-gather.12 = f32[128,4,128]{2,1,0:T(4,128)S(1)} all-gather(f32[1,4,128]{2,1,0:T(4,128)S(1)} %fusion.33), channel_id=6, replica_groups=mesh['leaf'=128] {'leaf'}, dimensions={0}, use_global_device_ids=true | all-gather | bytes 264192 | tf_op jit(solution)/shard_map/all_gather | solution.py:45
  568.5 33.3 %all-gather.13 = f32[128,4,128]{2,1,0:T(4,128)S(1)} all-gather(f32[1,4,128]{2,1,0:T(4,128)S(1)} %fusion.32), channel_id=7, replica_groups=mesh['leaf'=128] {'leaf'}, dimensions={0}, use_global_device_ids=true | all-gather | bytes 264192 | tf_op jit(solution)/shard_map/all_gather | solution.py:45
  601.9 33.3 %all-gather.14 = f32[128,4,128]{2,1,0:T(4,128)S(1)} all-gather(f32[1,4,128]{2,1,0:T(4,128)S(1)} %fusion.31), channel_id=8, replica_groups=mesh['leaf'=128] {'leaf'}, dimensions={0}, use_global_device_ids=true | all-gather | bytes 264192 | tf_op jit(solution)/shard_map/all_gather | solution.py:45
  635.3 33.4 %all-gather.15 = bf16[128,4,128]{2,1,0:T(4,128)(2,1)S(1)} all-gather(bf16[1,4,128]{2,1,0:T(4,128)(2,1)S(1)} %fusion.30), channel_id=9, replica_groups=mesh['leaf'=128] {'leaf'}, dimensions={0}, use_global_device_ids=true | all-gather | bytes 132096 | tf_op jit(solution)/shard_map/all_gather | solution.py:45
  687.5 46.6 %all-gather.39.cloned.1.call-done = bf16[128,32,128]{2,1,0:T(8,128)(2,1)} async-done(((bf16[1,32,128]{2,1,0:T(8,128)(2,1)}), bf16[128,32,128]{2,1,0:T(8,128)(2,1)}) %all-gather.39.cloned.1.call-update) | async-done | bytes 1048592 | tf_op jit(solution)/shard_map/all_gather | solution.py:46
  745.8 220.2 %while.10 = (s32[]{:T(128)}, f32[16,2,4,256]{3,2,1,0:T(4,128)}, s32[16,2,16]{2,1,0:T(2,128)S(1)}, bf16[96,36,256]{2,1,0:T(8,128)(2,1)}, bf16[16,2,32,256]{3,2,1,...) while((s32[]{:T(128)}, f32[16,2,4,256]{3,2,1,0:T(4,128)}, ...), condition=%wide.region_4.6_spmd, body=%wide.region_0.5_spmd.sunk | while | flops 324570912 | bytes 4859501 | solution.py:119
  756.0 3.6 fusion.101
  764.4 2.9 fusion.100
  769.8 3.6 fusion.101
  778.2 2.9 fusion.100
  783.6 3.6 fusion.101
  792.0 2.9 fusion.100
  797.3 3.6 fusion.101
  805.7 3.0 fusion.100
  811.1 3.5 fusion.101
  819.5 2.9 fusion.100
  824.9 3.5 fusion.101
  833.2 2.9 fusion.100
  838.6 3.6 fusion.101
  847.0 2.9 fusion.100
  852.4 3.5 fusion.101
  860.8 2.9 fusion.100
  866.1 3.6 fusion.101
  874.5 3.0 fusion.100
  879.9 3.5 fusion.101
  888.3 2.9 fusion.100
  893.7 3.6 fusion.101
  902.1 3.0 fusion.100
  907.4 3.5 fusion.101
  915.8 3.0 fusion.100
  921.2 3.5 fusion.101
  929.6 2.9 fusion.100
  934.9 3.6 fusion.101
  943.4 2.9 fusion.100
  948.7 3.6 fusion.101
  957.1 3.0 fusion.100
  962.5 3.5 fusion.101
  (322 shorter events, 175.4 us)
Async XLA Ops:
  6.5 335.8 %copy-start = (bf16[32,128,256]{2,1,0:T(8,128)(2,1)S(1)}, bf16[32,128,256]{2,1,0:T(8,128)(2,1)}, u32[]{:S(2)}) copy-start(bf16[32,128,256]{2,1,0:T(8,128)(2,1)} %param.15) | copy-start | bytes 6291460
  6.5 7.5 copy-start.14
  6.5 73.6 %all-gather.25.cloned.1.call-start = ((), (), s32[]{:S(2)}) async-start(), calls=%async_computation | async-start | bytes 1056768 | tf_op jit(solution)/shard_map/all_gather | solution.py:46
  8.0 329.7 %copy-start.2 = (bf16[32,32,256]{2,1,0:T(8,128)(2,1)S(1)}, bf16[32,32,256]{2,1,0:T(8,128)(2,1)}, u32[]{:S(2)}) copy-start(bf16[32,32,256]{2,1,0:T(8,128)(2,1)} %param.13) | copy-start | bytes 1572868
  8.0 330.0 %copy-start.11 = (bf16[32,4,256]{2,1,0:T(4,128)(2,1)S(1)}, bf16[32,4,256]{2,1,0:T(4,128)(2,1)}, u32[]{:S(2)}) copy-start(bf16[32,4,256]{2,1,0:T(4,128)(2,1)} %param.14) | copy-start | bytes 196612
  14.0 130.0 %all-gather.27.cloned.1.call-start = ((), (), s32[]{:S(2)}) async-start(), calls=%async_computation.1 | async-start | bytes 1056768 | tf_op jit(solution)/shard_map/all_gather | solution.py:46
  14.1 385.8 %copy-start.13 = (s32[1024]{0:T(1024)}, s32[1024]{0:T(1024)S(1)}, u32[]{:S(2)}) copy-start(s32[1024]{0:T(1024)S(1)} %pad_clamp_fusion.2) | copy-start | bytes 12292
  14.1 386.4 %copy-start.12 = (pred[128]{0:T(512)(128)(4,1)}, pred[128]{0:T(512)(128)(4,1)S(1)}, u32[]{:S(2)}) copy-start(pred[128]{0:T(512)(128)(4,1)S(1)} %and_bitcast_fusion) | copy-start | bytes 388
  82.5 125.4 %all-gather.29.cloned.1.call-start = ((), (), s32[]{:S(2)}) async-start(), calls=%async_computation.2 | async-start | bytes 1056768 | tf_op jit(solution)/shard_map/all_gather | solution.py:46
  146.4 125.2 %all-gather.31.cloned.1.call-start = ((), (), s32[]{:S(2)}) async-start(), calls=%async_computation.3 | async-start | bytes 1056768 | tf_op jit(solution)/shard_map/all_gather | solution.py:46
  210.2 125.1 %all-gather.33.cloned.1.call-start = ((), (), s32[]{:S(2)}) async-start(), calls=%async_computation.4 | async-start | bytes 1056768 | tf_op jit(solution)/shard_map/all_gather | solution.py:46
  273.9 125.1 %all-gather.35.cloned.1.call-start = ((), (), s32[]{:S(2)}) async-start(), calls=%async_computation.5 | async-start | bytes 1056768 | tf_op jit(solution)/shard_map/all_gather | solution.py:46
  337.6 332.1 %all-gather.37.cloned.1.call-start = ((), (), s32[]{:S(2)}) async-start(), calls=%async_computation.6 | async-start | bytes 1056768 | tf_op jit(solution)/shard_map/all_gather | solution.py:46
  338.0 96.8 %copy-start.1 = (bf16[1,128,256]{2,1,0:T(8,128)(2,1)S(1)}, bf16[1,128,256]{2,1,0:T(8,128)(2,1)}, u32[]{:S(2)}) copy-start(bf16[1,128,256]{2,1,0:T(8,128)(2,1)} %param.17) | copy-start | bytes 196612
  338.0 345.9 %collective-permute-start = (bf16[32,36,256]{2,0,1:T(8,128)(2,1)S(1)}, bf16[32,36,256]{2,0,1:T(8,128)(2,1)}, u32[]{:S(2)}, u32[]{:S(2)}) collective-permute-start(bf16[32,36,256]{2,0,1:T(8,128)(2,1)S(1)} %copy_dynamic-update-slice_fusion.1), channel_id=1, source_target_pairs={{0,1},{1,2},{2,3},{3,4},{4,5},{5,6},{6,7},{7,8},{8,9},{9,10},{10,1... | collective-permute-start | bytes 1769480 | tf_op jit(solution)/shard_map/ppermute | solution.py:16
  341.0 342.9 %collective-permute-start.1 = (bf16[32,36,256]{2,0,1:T(8,128)(2,1)S(1)}, bf16[32,36,256]{2,0,1:T(8,128)(2,1)}, u32[]{:S(2)}, u32[]{:S(2)}) collective-permute-start(bf16[32,36,256]{2,0,1:T(8,128)(2,1)S(1)} %copy_dynamic-update-slice_fusion.1), channel_id=1, source_target_pairs={{1,0},{2,1},{3,2},{4,3},{5,4},{6,5},{7,6},{8,7},{9,8},{10,9},{11,1... | collective-permute-start | bytes 1769480 | tf_op jit(solution)/shard_map/ppermute | solution.py:17
  342.3 1.2 copy-start.4
  401.4 332.8 %all-gather.39.cloned.1.call-start = ((), (), s32[]{:S(2)}) async-start(), calls=%async_computation.7 | async-start | bytes 1056768 | tf_op jit(solution)/shard_map/all_gather | solution.py:46
  468.2 167.0 %copy-start.5 = (f32[128,4,128]{2,1,0:T(4,128)}, f32[128,4,128]{2,1,0:T(4,128)S(1)}, u32[]{:S(2)}) copy-start(f32[128,4,128]{2,1,0:T(4,128)S(1)} %all-gather.9) | copy-start | bytes 786436
  501.6 167.1 %copy-start.6 = (f32[128,4,128]{2,1,0:T(4,128)}, f32[128,4,128]{2,1,0:T(4,128)S(1)}, u32[]{:S(2)}) copy-start(f32[128,4,128]{2,1,0:T(4,128)S(1)} %all-gather.10) | copy-start | bytes 786436
  535.0 134.2 %copy-start.7 = (f32[128,4,128]{2,1,0:T(4,128)}, f32[128,4,128]{2,1,0:T(4,128)S(1)}, u32[]{:S(2)}) copy-start(f32[128,4,128]{2,1,0:T(4,128)S(1)} %all-gather.11) | copy-start | bytes 786436
  568.4 100.8 %copy-start.8 = (f32[128,4,128]{2,1,0:T(4,128)}, f32[128,4,128]{2,1,0:T(4,128)S(1)}, u32[]{:S(2)}) copy-start(f32[128,4,128]{2,1,0:T(4,128)S(1)} %all-gather.12) | copy-start | bytes 786436
  601.8 67.4 %copy-start.9 = (f32[128,4,128]{2,1,0:T(4,128)}, f32[128,4,128]{2,1,0:T(4,128)S(1)}, u32[]{:S(2)}) copy-start(f32[128,4,128]{2,1,0:T(4,128)S(1)} %all-gather.13) | copy-start | bytes 786436
  635.2 34.1 %copy-start.10 = (f32[128,4,128]{2,1,0:T(4,128)}, f32[128,4,128]{2,1,0:T(4,128)S(1)}, u32[]{:S(2)}) copy-start(f32[128,4,128]{2,1,0:T(4,128)S(1)} %all-gather.14) | copy-start | bytes 786436
  734.1 10.6 %copy-start.3 = (bf16[128,32,128]{2,1,0:T(8,128)(2,1)S(1)}, bf16[128,32,128]{2,1,0:T(8,128)(2,1)}, u32[]{:S(2)}) copy-start(bf16[128,32,128]{2,1,0:T(8,128)(2,1)} %all-gather.25.cloned.1.call-done) | copy-start | bytes 3145732
Sparse Core Ops, SparseCore 0:
  14.1 65.9 all-gather.24
  82.9 61.0 all-gather.26
  146.8 61.0 all-gather.28
  210.5 61.0 all-gather.30
  274.2 61.0 all-gather.32
  337.9 61.0 all-gather.34
  401.8 61.1 all-gather.36
  673.7 60.3 all-gather.38
where the time goes:
time: 977 us; the launch traced here: 973 us
  waiting for transfers between devices  413 us (42%)
  blocking collectives  266 us (27%)
  local copies, waits for them, and re-layouts  145 us (15%)
  matrix products  106 us (11%)
  other arithmetic  23.2 us (2%)
  between operations  13.8 us (1%)
    all_gather x8, waiting for transfers between devices, collect_level(): lax.all_gather(own_x[None], 'leaf', axis=0, tiled=True)  413 us
    all_gather x8, blocking collectives, collect_level(): lax.all_gather(own_w[None], 'leaf', axis=0, tiled=True)  266 us
    dot_general x32, matrix products, kernel_apply(): jnp.einsum('tms,mrs->rt', kern, source_w, preferred_element_type=jnp.floa...  104 us
    gather x32, local copies, waits for them, and re-layouts, one_leaf(): far = kernel_apply(target, table_xb[far_ids], table_wb[far_ids])  61.6 us
    gather x16, local copies, waits for them, and re-layouts, one_leaf(): sources = padded[near_ids]  34.4 us
    unnamed x47, local copies, waits for them, and re-layouts  21.4 us
  transfers between devices with their start and end apart: 10, of which 7 were waited for; matrix products, arithmetic and copies ran while one was open for 2% of the time, Pallas kernels for 0%

commit v1 on v0

v1 whole, which is shorter than its diff:
```python
import functools
import math

import jax
import jax.numpy as jnp
from jax import lax
from jax.experimental import pallas as pl
from jax.experimental.pallas import tpu as pltpu
from jax.sharding import PartitionSpec as P

gauss = 0.0625
bf16 = jnp.bfloat16
f32 = jnp.float32
NT = (((1,), (1,)), ((), ()))
FACTOR = 2.0 * gauss * math.log2(math.e)
WIDE = 128
GROUP = 8
SIDE = 4
VMEM = pl.BlockSpec(memory_space=pltpu.VMEM)
SMEM = pl.BlockSpec(memory_space=pltpu.SMEM)
PARAMS = pltpu.CompilerParams(vmem_limit_bytes=60 << 20)


def pieces(x):
    a = x.astype(bf16)
    r = x - a.astype(f32)
    b = r.astype(bf16)
    c = (r - b.astype(f32)).astype(bf16)
    return a, b, c


def norm_pieces(x):
    y = x.astype(f32)
    return pieces(-0.5 * jnp.sum(y * y, axis=0, keepdims=True))


def form_rows(x, first, second):
    dims, n = x.shape
    at = lax.broadcasted_iota(jnp.int32, (16, n), 0)
    tail = jnp.zeros((16, n), f32)
    for k in range(3):
        tail = jnp.where(at == k, first[k], tail)
        tail = jnp.where(at == 3 + k, second[k], tail)
    return jnp.concatenate([x, tail.astype(bf16), jnp.zeros((WIDE - dims - 16, n), bf16)], axis=0)


def source_form(x, eye):
    norms = [p.astype(f32) for p in norm_pieces(x)]
    block = form_rows(x, [1.0] * 3, norms)
    return lax.dot_general(eye, block, NT, preferred_element_type=f32).astype(bf16)


def target_form(x):
    norms = [p.astype(f32) for p in norm_pieces(x)]
    return form_rows(x, norms, [1.0] * 3)


def eye_of(n):
    return (
        lax.broadcasted_iota(jnp.int32, (n, n), 0) == lax.broadcasted_iota(jnp.int32, (n, n), 1)
    ).astype(f32).astype(bf16)


def apply_map(three, maps):
    m = three.shape[0] // 3
    out = lax.dot_general(three, maps, NT, preferred_element_type=f32)
    return out[:m] + (out[m : 2 * m] + out[2 * m :])


def blocks_apply(target, sources, ws):
    p = jnp.dot(jnp.concatenate(sources, axis=0), target, preferred_element_type=f32)
    kern = jnp.exp2(p * FACTOR).astype(bf16)
    return jnp.dot(jnp.concatenate(ws, axis=1), kern, preferred_element_type=f32)


def upward_kernel(points, weights, leaf_maps, root_maps, picks, root_w, root_x, stacked):
    per, dims, leaf_size = points.shape
    rank = leaf_maps.shape[1]
    want = picks[...]
    x = jnp.zeros((dims, rank), f32)
    for g in range(per):
        w = lax.dot_general(weights[g], leaf_maps[g], NT, preferred_element_type=f32)
        stacked[:, g * rank : (g + 1) * rank] = w
        at = lax.broadcasted_iota(jnp.int32, (leaf_size, rank), 0) + g * leaf_size
        hot = (at == want).astype(f32).astype(bf16)
        x = x + jnp.dot(points[g], hot, preferred_element_type=f32)
    w = apply_map(jnp.concatenate(pieces(stacked[...]), axis=0), root_maps[0])
    root_w[0] = jnp.concatenate(pieces(w), axis=0)
    root_x[0] = x.astype(bf16)


def upward(points, weights, leaf_maps, root_maps, root_picks):
    per, dims, _ = points.shape
    rhs, rank = weights.shape[1], leaf_maps.shape[1]
    return pl.pallas_call(
        upward_kernel,
        in_specs=[VMEM] * 5,
        out_specs=[VMEM] * 2,
        out_shape=[
            jax.ShapeDtypeStruct((1, 3 * rhs, rank), bf16),
            jax.ShapeDtypeStruct((1, dims, rank), bf16),
        ],
        scratch_shapes=[pltpu.VMEM((rhs, per * rank), f32)],
        compiler_params=PARAMS,
    )(points, weights, leaf_maps, root_maps, root_picks)


def merge(left, right, maps):
    three = jnp.concatenate([left, right], axis=1)
    return jnp.concatenate(pieces(apply_map(three, maps)), axis=0)


def group_kernel(roots, maps, out):
    rhs = roots.shape[1] // 3
    level = [roots[i] for i in range(GROUP)]
    nodes = list(level)
    slot = 0
    while len(level) > 1:
        level = [
            merge(level[2 * i], level[2 * i + 1], maps[slot + i]) for i in range(len(level) // 2)
        ]
        slot += len(level)
        nodes += level
    rows = [node[:rhs] for node in nodes] + [nodes[-1][rhs:]]
    rows.append(jnp.zeros((out.shape[1] - (len(nodes) + 2) * rhs, rows[0].shape[1]), bf16))
    out[0] = jnp.concatenate(rows, axis=0)


def slab_kernel(groups, maps, out):
    top = 2 * GROUP - 2
    rhs = out.shape[1] // 6
    level = [groups[i, top * rhs : (top + 3) * rhs] for i in range(SIDE)]
    a = merge(level[0], level[1], maps[0])
    b = merge(level[2], level[3], maps[1])
    c = merge(a, b, maps[2])
    out[0] = jnp.concatenate([a[:rhs], b[:rhs], c, jnp.zeros((rhs, c.shape[1]), bf16)], axis=0)


def merged(kernel, rows, inputs, maps):
    return pl.pallas_call(
        kernel,
        in_specs=[VMEM] * 2,
        out_specs=VMEM,
        out_shape=jax.ShapeDtypeStruct((1, rows, inputs.shape[-1]), bf16),
        compiler_params=PARAMS,
    )(inputs, maps)


def near_kernel(unroll, lists, points, first, second, w_own, w_first, w_second, out, targets, sources, ws):
    per, dims, leaf_size = points.shape
    near = lists.shape[1]
    eye = eye_of(leaf_size)
    for i, (ref, w_ref) in enumerate(((points, w_own), (first, w_first), (second, w_second))):

        def prepare(g, carry, i=i, ref=ref, w_ref=w_ref):
            sources[i * per + g] = source_form(ref[g], eye)
            ws[i * per + g] = w_ref[g]
            if i == 0:
                targets[g] = target_form(ref[g])
            return carry

        lax.fori_loop(0, per, prepare, 0, unroll=4)

    def leaves(step, carry):
        for u in range(unroll):
            g = step * unroll + u
            target = targets[g]
            total = jnp.zeros(out.shape[1:], f32)
            for j in range(0, near, 4):
                ids = [lists[g, j + k] for k in range(4)]
                total = total + blocks_apply(target, [sources[h] for h in ids], [ws[h] for h in ids])
            out[g] = total
        return carry

    lax.fori_loop(0, per // unroll, leaves, 0)


def near_field(slots, points, first, second, w_own, w_first, w_second):
    per, dims, leaf_size = points.shape
    rhs = w_own.shape[1]
    return pl.pallas_call(
        functools.partial(near_kernel, 4),
        in_specs=[SMEM] + [VMEM] * 6,
        out_specs=[VMEM] * 2,
        out_shape=[
            jax.ShapeDtypeStruct((per, rhs, leaf_size), f32),
            jax.ShapeDtypeStruct((per, WIDE, leaf_size), bf16),
        ],
        scratch_shapes=[
            pltpu.VMEM((3 * per, leaf_size, WIDE), bf16),
            pltpu.VMEM((3 * per, rhs, leaf_size), bf16),
        ],
        compiler_params=PARAMS,
    )(slots, points, first, second, w_own, w_first, w_second)


def far_kernel(unroll, lists, groups, slabs, maps, root_x, picks, targets, near, out, x_all, sources, ws):
    nodes, dims, rank = root_x.shape
    per, fars = lists.shape
    rhs = out.shape[1]
    eye = eye_of(2 * rank)

    tops = []
    for y in range(SIDE):
        for z in range(SIDE):
            group = SIDE * y + z
            row = 0
            count = GROUP
            while count:
                base = count * SIDE * SIDE + count * group
                for i in range(count):
                    ws[base + i] = groups[y, z, row : row + rhs]
                    row += rhs
                count //= 2
        ws[2 * SIDE + 2 * y] = slabs[y, 0, :rhs]
        ws[2 * SIDE + 2 * y + 1] = slabs[y, 0, rhs : 2 * rhs]
        ws[SIDE + y] = slabs[y, 0, 2 * rhs : 3 * rhs]
        tops.append(slabs[y, 0, 2 * rhs : 5 * rhs])
    a = merge(tops[0], tops[1], maps[0])
    b = merge(tops[2], tops[3], maps[1])
    ws[2] = a[:rhs]
    ws[3] = b[:rhs]
    ws[1] = merge(a, b, maps[2])[:rhs]
    ws[0] = jnp.zeros((rhs, rank), bf16)

    def copy_root(n, carry):
        x_all[nodes + n] = root_x[n]
        return carry

    lax.fori_loop(0, nodes, copy_root, 0, unroll=8)
    x_all[0] = jnp.zeros((dims, rank), bf16)
    half = nodes // 2
    while half:

        def select(i, carry, half=half):
            n = half + i
            pair = jnp.concatenate([x_all[2 * n], x_all[2 * n + 1]], axis=1)
            at = lax.broadcasted_iota(jnp.int32, (2 * rank, rank), 0)
            hot = (at == picks[n]).astype(f32).astype(bf16)
            x_all[n] = jnp.dot(pair, hot, preferred_element_type=f32).astype(bf16)
            return carry

        lax.fori_loop(0, half, select, 0, unroll=min(half, 8))
        half //= 2

    def prepare(i, carry):
        pair = jnp.concatenate([x_all[2 * i], x_all[2 * i + 1]], axis=1)
        form = source_form(pair, eye)
        sources[2 * i] = form[:rank]
        sources[2 * i + 1] = form[rank:]
        return carry

    lax.fori_loop(0, nodes, prepare, 0, unroll=4)

    def leaves(step, carry):
        for u in range(unroll):
            g = step * unroll + u
            target = targets[g]
            total = near[g]
            for j in range(0, fars, 8):
                ids = [lists[g, j + k] for k in range(8)]
                total = total + blocks_apply(target, [sources[n] for n in ids], [ws[n] for n in ids])
            out[g] = total
        return carry

    lax.fori_loop(0, per // unroll, leaves, 0)


def far_field(far_lists, groups, slabs, maps, root_x, picks, targets, near):
    nodes, dims, rank = root_x.shape
    rhs = near.shape[1]
    return pl.pallas_call(
        functools.partial(far_kernel, 4),
        in_specs=[SMEM] + [VMEM] * 7,
        out_specs=VMEM,
        out_shape=jax.ShapeDtypeStruct(near.shape, f32),
        scratch_shapes=[
            pltpu.VMEM((2 * nodes, dims, rank), bf16),
            pltpu.VMEM((2 * nodes, rank, WIDE), bf16),
            pltpu.VMEM((2 * nodes, rhs, rank), bf16),
        ],
        compiler_params=PARAMS,
    )(far_lists, groups, slabs, maps, root_x, picks[:, None, :], targets, near)


def home_of(node):
    if node >= 64:
        return GROUP * ((node - 64) // 4) + (node - 64) % 4
    if node >= 32:
        return GROUP * ((node - 32) // 2) + 4 + (node - 32) % 2
    if node >= 16:
        return GROUP * (node - 16) + 6
    if node >= 8:
        y, z = (node - 8) // 2, (node - 8) % 2
    elif node >= 4:
        y, z = node - 4, 2
    else:
        y, z = {2: 0, 3: 1, 1: 2, 0: 3}[node], 3
    return GROUP * (SIDE * y + z) + 7


def gather_over(x, inner, count, size):
    groups = [
        [outer + inner * k + low for k in range(count)]
        for outer in range(0, size, inner * count)
        for low in range(inner)
    ]
    return lax.all_gather(x, "leaf", axis=0, tiled=True, axis_index_groups=groups)


def on_device(
    points, weights, leaf_maps, root_maps, top_maps, root_picks, top_picks, near_lists, far_lists
):
    per, dims, leaf_size = points.shape
    rhs = weights.shape[1]
    size = lax.axis_size("leaf")
    me = lax.axis_index("leaf")
    over_group = functools.partial(gather_over, inner=1, count=GROUP, size=size)
    over_z = functools.partial(gather_over, inner=GROUP, count=SIDE, size=size)
    over_y = functools.partial(gather_over, inner=GROUP * SIDE, count=SIDE, size=size)

    placed = lax.ppermute(top_maps, "leaf", [(n, home_of(n)) for n in range(size)])
    pairs = [(i, i ^ 1) for i in range(size)]
    bridges = [(i, i + 1) for i in range(1, size - 1, 2)]
    bridges = bridges + [(j, i) for i, j in bridges]
    first = lax.ppermute(points, "leaf", pairs)
    w_first = lax.ppermute(weights, "leaf", pairs)
    second = lax.ppermute(points, "leaf", bridges)
    w_second = lax.ppermute(weights, "leaf", bridges)

    picks = lax.all_gather(top_picks, "leaf", axis=0, tiled=True)
    group_maps = over_group(placed)
    slab_maps = over_z(group_maps[GROUP - 1 :])
    top_maps_all = over_y(slab_maps[SIDE - 1 :])
    root_w, root_x = upward(points, weights, leaf_maps, root_maps, root_picks)
    group_w = over_group(root_w)
    x_all = over_y(over_z(over_group(root_x)))
    group_nodes = merged(group_kernel, 18 * rhs, group_w, group_maps)
    slab_groups = over_z(group_nodes)
    slab_nodes = merged(slab_kernel, 6 * rhs, slab_groups, slab_maps)
    groups = over_y(slab_groups[None])
    slabs = over_y(slab_nodes[None])

    local = near_lists - me * per
    side = jnp.where(me % 2 == 0, jnp.where(local < 0, 2, 1), jnp.where(local < 0, 1, 2))
    inside = jnp.logical_and(local >= 0, local < per)
    slots = jnp.where(inside, local, side * per + local % per)
    near, targets = near_field(slots, points, first, second, weights, w_first, w_second)
    return far_field(far_lists, groups, slabs, top_maps_all, x_all, picks, targets, near)


def solution(mesh):
    leaf3 = P("leaf", None, None)
    leaf2 = P("leaf", None)
    return jax.shard_map(
        on_device,
        mesh=mesh,
        in_specs=(leaf3,) * 5 + (leaf2,) * 4,
        out_specs=leaf3,
        check_vma=False,
    )
```

time: 977 us -> 310 us (0.32)
  waiting for transfers between devices: 413 us -> 0.03 us
  local copies, waits for them, and re-layouts: 145 us -> 2.47 us
  Pallas kernels: 0 us -> 127 us
  blocking collectives: 266 us -> 156 us
  matrix products: 106 us -> 0 us
  other arithmetic: 23.2 us -> 0.62 us
    all_gather x8 -> x1, waiting for transfers between devices: 413 us -> 0.01 us  [gather_over(): lax.all_gather(x, 'leaf', axis=0, tiled=True, axis_index_groups=groups)]
    pallas_call x0 -> x5, Pallas kernels: none -> 127 us  [the longest x1 81 us: far_field(): pl.pallas_call(functools.partial(far_kernel, 4), in_specs=[SMEM] + [VMEM]...]
    all_gather x8 -> x10, blocking collectives: 266 us -> 156 us  [the longest x9 126 us: gather_over(): lax.all_gather(x, 'leaf', axis=0, tiled=True, axis_index_groups=groups)]
    dot_general x41 -> x0, matrix products: 106 us -> none  [the longest x32 104 us: kernel_apply(): jnp.einsum('tms,mrs->rt', kern, source_w, preferred_element_type=jnp.floa...]
    gather x57 -> x0, local copies, waits for them, and re-layouts: 104 us -> none  [the longest x32 61.6 us: one_leaf(): far = kernel_apply(target, table_xb[far_ids], table_wb[far_ids])]
    unnamed x47 -> x23, local copies, waits for them, and re-layouts: 21.4 us -> 2.46 us
    select_n x40 -> x1, other arithmetic: 13.1 us -> 0.62 us  [on_device(): slots = jnp.where(inside, local, side * per + local % per)]
  transfers between devices with their start and end apart: 10 -> 6, of which waited for: 7 -> 0; matrix products, arithmetic and copies ran while one was open for 2% -> 0% of each run, Pallas kernels for 0% -> 13%
where the time goes in v1:
time: 310 us
  blocking collectives  156 us (50%)
  Pallas kernels  127 us (41%)
  between operations  13.5 us (4%)
  starting transfers between devices  10.4 us (3%)
    all_gather x9, blocking collectives, gather_over(): lax.all_gather(x, 'leaf', axis=0, tiled=True, axis_index_groups=groups)  126 us
    pallas_call x1, Pallas kernels, far_field(): pl.pallas_call(functools.partial(far_kernel, 4), in_specs=[SMEM] + [VMEM]...  81 us
    pallas_call x1, Pallas kernels, near_field(): pl.pallas_call(functools.partial(near_kernel, 4), in_specs=[SMEM] + [VMEM...  37.8 us
    all_gather x1, blocking collectives, on_device(): picks = lax.all_gather(top_picks, 'leaf', axis=0, tiled=True)  29.8 us
    ppermute x1, starting transfers between devices, on_device(): lax.ppermute(top_maps, 'leaf', [(n, home_of(n)) for n in range(size)])  6.32 us
  transfers between devices with their start and end apart: 6, of which 0 were waited for; matrix products, arithmetic and copies ran while one was open for 0% of the time, Pallas kernels for 13%

profile of v1, /device:TPU:0, one launch (start us, length us, event | category | flops | bytes accessed | tf_op | source)
XLA Modules:
  0.0 309.6 jit_solution(8170279625330796330)
XLA Ops:
  6.5 0.0 copy-start.1
  6.5 0.0 copy-start.5
  6.5 0.0 copy-start.10
  6.5 0.0 copy-start.8
  6.5 0.0 copy-start.9
  6.5 0.0 all-gather.5.cloned.1.call-start
  6.6 4.2 %shard_map.91 = (bf16[1,12,128]{2,1,0:T(8,128)(2,1)}, bf16[1,32,128]{2,1,0:T(8,128)(2,1)}) custom-call(bf16[32,32,256]{2,1,0:T(8,128)(2,1)} %points.3, bf16[32,4,256]{2,1,0:T(4,128)(2,1)} %w_own.1, bf16[32,128,256]{2,1,0:T(8,128)(2,1)} %leaf_maps.1, bf16[1,128,4096]{2,1,0:T(8,128)(2,1)} %root_maps.1, s32[1,128]{1,0:T(1,128)} %picks.1), custom_call_target="tpu_custom_call" | custom-call | tf_op jit(solution)/shard_map/pallas_call | solution.py:95
  10.8 13.4 %all_gather.40 = bf16[8,32,128]{2,1,0:T(8,128)(2,1)S(1)} all-gather(bf16[1,32,128]{2,1,0:T(8,128)(2,1)} %get-tuple-element.10), channel_id=1, replica_groups={{0,1,2,3,4,5,6,7},{8,9,10,11,12,13,14,15},{16,17,18,19,20,21,22,23},{24..., dimensions={0}, use_global_device_ids=true | all-gather | bytes 73728 | tf_op jit(solution)/shard_map/all_gather | solution.py:308
  24.1 14.2 %all_gather.41 = bf16[32,32,128]{2,1,0:T(8,128)(2,1)} all-gather(bf16[8,32,128]{2,1,0:T(8,128)(2,1)S(1)} %all_gather.40), channel_id=1, replica_groups={{0,8,16,24},{1,9,17,25},{2,10,18,26},{3,11,19,27},{4,12,20,28},{5,13,21..., dimensions={0}, use_global_device_ids=true | all-gather | bytes 327680 | tf_op jit(solution)/shard_map/all_gather | solution.py:308
  38.3 0.0 all-gather.5.cloned.1.call-update
  38.3 0.0 copy-done.1
  38.4 0.1 collective-permute-start.1
  38.5 0.7 collective-permute-start.2
  39.2 0.0 copy-done.5
  39.2 2.6 collective-permute-start.3
  41.8 0.7 collective-permute-start.4
  42.4 0.0 copy-done.10
  42.5 6.3 %collective-permute-start = (bf16[1,128,256]{2,1,0:T(8,128)(2,1)S(1)}, bf16[1,128,256]{2,1,0:T(8,128)(2,1)S(1)}, u32[]{:S(2)}, u32[]{:S(2)}) collective-permute-start(bf16[1,128,256]{2,1,0:T(8,128)(2,1)S(1)} %copy-done.10), channel_id=1, source_target_pairs={{0,127},{1,95},{2,31},{3,63},{4,23},{5,55},{6,87},{7,119},{8,7},{9... | collective-permute-start | bytes 196616 | tf_op jit(solution)/shard_map/ppermute | solution.py:322
  48.8 0.0 copy-done.8
  48.8 0.1 copy.11
  48.9 0.6 fusion.2.lists
  49.5 18.5 %all_gather.33.roots = bf16[8,12,128]{2,1,0:T(8,128)(2,1)} all-gather(bf16[1,12,128]{2,1,0:T(8,128)(2,1)} %get-tuple-element.9), channel_id=1, replica_groups={{0,1,2,3,4,5,6,7},{8,9,10,11,12,13,14,15},{16,17,18,19,20,21,22,23},{24..., dimensions={0}, use_global_device_ids=true | all-gather | bytes 27648 | tf_op jit(solution)/shard_map/all_gather | solution.py:308
  68.0 0.0 copy-done.9
  68.0 29.8 %all-gather.2.picks = s32[128,1,128]{2,1,0:T(1,128)} all-gather(s32[1,1,128]{2,1,0:T(1,128)S(1)} %bitcast.5), channel_id=1, replica_groups=mesh['leaf'=128] {'leaf'}, dimensions={0}, use_global_device_ids=true | all-gather | bytes 66048 | tf_op jit(solution)/shard_map/all_gather | solution.py:331
  97.8 0.0 collective-permute-done
  97.8 13.1 %all_gather.34.maps = bf16[8,128,256]{2,1,0:T(8,128)(2,1)S(1)} all-gather(bf16[1,128,256]{2,1,0:T(8,128)(2,1)S(1)} %collective-permute-done), channel_id=1, replica_groups={{0,1,2,3,4,5,6,7},{8,9,10,11,12,13,14,15},{16,17,18,19,20,21,22,23},{24..., dimensions={0}, use_global_device_ids=true | all-gather | bytes 589824 | tf_op jit(solution)/shard_map/all_gather | solution.py:308
  110.9 0.0 copy-start
  110.9 0.8 copy-done
  111.7 2.1 shard_map.92
  113.8 12.9 %all_gather.37.maps = bf16[4,128,256]{2,1,0:T(8,128)(2,1)S(1)} all-gather(bf16[1,128,256]{2,1,0:T(8,128)(2,1)S(1)} %slice.8), channel_id=1, replica_groups={{0,8,16,24},{1,9,17,25},{2,10,18,26},{3,11,19,27},{4,12,20,28},{5,13,21..., dimensions={0}, use_global_device_ids=true | all-gather | bytes 327680 | tf_op jit(solution)/shard_map/all_gather | solution.py:308
  126.8 14.2 %all_gather.35.groups = bf16[4,72,128]{2,1,0:T(8,128)(2,1)} all-gather(bf16[1,72,128]{2,1,0:T(8,128)(2,1)} %shard_map.92), channel_id=1, replica_groups={{0,8,16,24},{1,9,17,25},{2,10,18,26},{3,11,19,27},{4,12,20,28},{5,13,21..., dimensions={0}, use_global_device_ids=true | all-gather | bytes 92160 | tf_op jit(solution)/shard_map/all_gather | solution.py:308
  141.0 0.0 copy-done.2
  141.0 1.9 shard_map.93
  142.9 12.8 %all-gather.1 = bf16[4,24,128]{2,1,0:T(8,128)(2,1)} all-gather(bf16[1,24,128]{2,1,0:T(8,128)(2,1)} %shard_map.93), channel_id=3, replica_groups={{0,32,64,96},{1,33,65,97},{2,34,66,98},{3,35,67,99},{4,36,68,100},{5,37..., dimensions={0}, use_global_device_ids=true | all-gather | bytes 30720 | tf_op jit(solution)/shard_map/all_gather | solution.py:308
  155.7 13.6 %all-gather = bf16[16,72,128]{2,1,0:T(8,128)(2,1)} all-gather(bf16[4,72,128]{2,1,0:T(8,128)(2,1)} %all_gather.35.groups), channel_id=2, replica_groups={{0,32,64,96},{1,33,65,97},{2,34,66,98},{3,35,67,99},{4,36,68,100},{5,37..., dimensions={0}, use_global_device_ids=true | all-gather | bytes 368640 | tf_op jit(solution)/shard_map/all_gather | solution.py:308
  169.3 13.2 %all_gather.39.maps = bf16[4,128,256]{2,1,0:T(8,128)(2,1)} all-gather(bf16[1,128,256]{2,1,0:T(8,128)(2,1)S(1)} %slice.9), channel_id=1, replica_groups={{0,32,64,96},{1,33,65,97},{2,34,66,98},{3,35,67,99},{4,36,68,100},{5,37..., dimensions={0}, use_global_device_ids=true | all-gather | bytes 327680 | tf_op jit(solution)/shard_map/all_gather | solution.py:308
  182.4 0.0 collective-permute-done.3.w_first
  182.4 0.0 collective-permute-done.4.w_second
  182.4 0.0 copy-start.7
  182.5 0.0 collective-permute-done.1.first
  182.5 0.0 copy-start.3
  182.5 0.0 collective-permute-done.2.second
  182.5 0.6 copy-done.6
  183.1 0.0 copy-done.7
  183.1 0.2 copy-done.3
  183.3 0.8 copy-done.4
  184.1 37.8 %shard_map.94 = (f32[32,4,256]{2,1,0:T(4,128)}, bf16[32,128,256]{2,1,0:T(8,128)(2,1)}) custom-call(s32[32,16]{1,0:T(8,128)} %fusion.2.lists, bf16[32,32,256]{2,1,0:T(8,128)(2,1)} %points.3, bf16[32,32,256]{2,1,0:T(8,128)(2,1)} %copy-done.3, bf16[32,32,256]{2,1,0:T(8,128)(2,1)} %copy-done.4, bf16[32,4,256]{2,1,0:T(4,128)(2,1)} %w_own.1, ...), custom_call_target="tpu_custom_call" | custom-call | tf_op jit(solution)/shard_map/pallas_call | solution.py:181
  221.8 81.0 %shard_map.95 = f32[32,4,256]{2,1,0:T(4,128)} custom-call(s32[32,32]{1,0:T(8,128)} %lists.1, bf16[4,4,72,128]{3,2,1,0:T(8,128)(2,1)} %bitcast.3, bf16[4,1,24,128]{3,2,1,0:T(8,128)(2,1)} %bitcast.4, bf16[4,128,256]{2,1,0:T(8,128)(2,1)} %all_gather.39.maps, bf16[128,32,128]{2,1,0:T(8,128)(2,1)} %all-gather.5.cloned.1.call-done.root_x, ...), custom_call_target="tpu_custom_call" | custom-call | tf_op jit(solution)/shard_map/pallas_call | solution.py:272
  (6 shorter events, 0.0 us)
Async XLA Ops:
  6.5 31.8 %copy-start.1 = (bf16[32,32,256]{2,1,0:T(8,128)(2,1)S(1)}, bf16[32,32,256]{2,1,0:T(8,128)(2,1)}, u32[]{:S(2)}) copy-start(bf16[32,32,256]{2,1,0:T(8,128)(2,1)} %points.3) | copy-start | bytes 1572868
  6.5 32.6 %copy-start.5 = (bf16[32,4,256]{2,1,0:T(4,128)(2,1)S(1)}, bf16[32,4,256]{2,1,0:T(4,128)(2,1)}, u32[]{:S(2)}) copy-start(bf16[32,4,256]{2,1,0:T(4,128)(2,1)} %w_own.1) | copy-start | bytes 196612
  6.5 35.9 %copy-start.10 = (bf16[1,128,256]{2,1,0:T(8,128)(2,1)S(1)}, bf16[1,128,256]{2,1,0:T(8,128)(2,1)}, u32[]{:S(2)}) copy-start(bf16[1,128,256]{2,1,0:T(8,128)(2,1)} %param.13) | copy-start | bytes 196612
  6.5 42.2 %copy-start.8 = (s32[32,16]{0,1:T(8,128)S(1)}, s32[32,16]{0,1:T(8,128)}, u32[]{:S(2)}) copy-start(s32[32,16]{0,1:T(8,128)} %param.16) | copy-start | bytes 6148
  6.5 61.4 %copy-start.9 = (s32[1,128]{1,0:T(1,128)S(1)}, s32[1,128]{1,0:T(1,128)}, u32[]{:S(2)}) copy-start(s32[1,128]{1,0:T(1,128)} %param.15) | copy-start | bytes 1540
  6.5 215.3 %all-gather.5.cloned.1.call-start = ((), (), s32[]{:S(2)}) async-start(), calls=%async_computation | async-start | bytes 1310720 | tf_op jit(solution)/shard_map/all_gather | solution.py:308
  38.4 144.1 %collective-permute-start.1 = (bf16[32,32,256]{2,1,0:T(8,128)(2,1)S(1)}, bf16[32,32,256]{2,1,0:T(8,128)(2,1)S(1)}, u32[]{:S(2)}, u32[]{:S(2)}) collective-permute-start(bf16[32,32,256]{2,1,0:T(8,128)(2,1)S(1)} %copy-done.1), channel_id=1, source_target_pairs={{0,1},{1,0},{2,3},{3,2},{4,5},{5,4},{6,7},{7,6},{8,9},{9,8},{10,11... | collective-permute-start | bytes 1572872 | tf_op jit(solution)/shard_map/ppermute | solution.py:326
  38.5 144.0 %collective-permute-start.2 = (bf16[32,32,256]{2,1,0:T(8,128)(2,1)S(1)}, bf16[32,32,256]{2,1,0:T(8,128)(2,1)S(1)}, u32[]{:S(2)}, u32[]{:S(2)}) collective-permute-start(bf16[32,32,256]{2,1,0:T(8,128)(2,1)S(1)} %copy-done.1), channel_id=1, source_target_pairs={{1,2},{3,4},{5,6},{7,8},{9,10},{11,12},{13,14},{15,16},{17,18},{19... | collective-permute-start | bytes 1572872 | tf_op jit(solution)/shard_map/ppermute | solution.py:328
  39.2 143.3 %collective-permute-start.3 = (bf16[32,4,256]{2,1,0:T(4,128)(2,1)S(1)}, bf16[32,4,256]{2,1,0:T(4,128)(2,1)S(1)}, u32[]{:S(2)}, u32[]{:S(2)}) collective-permute-start(bf16[32,4,256]{2,1,0:T(4,128)(2,1)S(1)} %copy-done.5), channel_id=1, source_target_pairs={{0,1},{1,0},{2,3},{3,2},{4,5},{5,4},{6,7},{7,6},{8,9},{9,8},{10,11... | collective-permute-start | bytes 196616 | tf_op jit(solution)/shard_map/ppermute | solution.py:327
  41.8 140.7 %collective-permute-start.4 = (bf16[32,4,256]{2,1,0:T(4,128)(2,1)S(1)}, bf16[32,4,256]{2,1,0:T(4,128)(2,1)S(1)}, u32[]{:S(2)}, u32[]{:S(2)}) collective-permute-start(bf16[32,4,256]{2,1,0:T(4,128)(2,1)S(1)} %copy-done.5), channel_id=1, source_target_pairs={{1,2},{3,4},{5,6},{7,8},{9,10},{11,12},{13,14},{15,16},{17,18},{19... | collective-permute-start | bytes 196616 | tf_op jit(solution)/shard_map/ppermute | solution.py:329
  42.5 55.3 %collective-permute-start = (bf16[1,128,256]{2,1,0:T(8,128)(2,1)S(1)}, bf16[1,128,256]{2,1,0:T(8,128)(2,1)S(1)}, u32[]{:S(2)}, u32[]{:S(2)}) collective-permute-start(bf16[1,128,256]{2,1,0:T(8,128)(2,1)S(1)} %copy-done.10), channel_id=1, source_target_pairs={{0,127},{1,95},{2,31},{3,63},{4,23},{5,55},{6,87},{7,119},{8,7},{9... | collective-permute-start | bytes 196616 | tf_op jit(solution)/shard_map/ppermute | solution.py:322
  110.9 0.8 copy-start
  126.8 14.2 %copy-start.2 = (bf16[4,128,256]{2,1,0:T(8,128)(2,1)}, bf16[4,128,256]{2,1,0:T(8,128)(2,1)S(1)}, u32[]{:S(2)}) copy-start(bf16[4,128,256]{2,1,0:T(8,128)(2,1)S(1)} %all_gather.37.maps) | copy-start | bytes 786436
  182.4 0.6 copy-start.6
  182.4 0.7 copy-start.7
  182.5 0.8 copy-start.3
  183.3 0.8 copy-start.4
Sparse Core Ops, SparseCore 0:
  38.5 27.1 all-gather.4
